TPU v7x, 32 devices: a whole 2x2x4 slice. The times are simulated.
32 devices in a mesh: section: 2 (over core), tensor: 2 (over x), dp: 8 (over z, y).
Axes of the slice: x: 2, y: 2, z: 4, core: 2. Of those that a mesh axis runs over, the one named last changes fastest.
Arguments:
- inputs: bfloat16 [16, 1024, 768], P('dp', 'tensor'), may hold values from -6 to 6
- segments: int32 [16, 1024], P('dp'), may hold values from 0 to 3, never falling along the last dimension, each value on 1 to 768 neighbouring positions
- cotangent: bfloat16 [16, 1024, 768], P('dp', 'tensor'), may hold values from -6 to 6
- norm_gains: bfloat16 [2, 2, 768], P('section'), may hold values from 0.5 to 1.5
- shared_biases: bfloat16 [2, 4, 768], P('section'), may hold values from -1.5 to 1.5
- w_qkv: bfloat16 [2, 768, 3, 768], P('section', None, None, 'tensor'), may hold values from -0.3125 to 0.3125
- qv_bias: bfloat16 [2, 2, 768], P('section', None, 'tensor'), may hold values from -1.5 to 1.5
- w_out: bfloat16 [2, 768, 768], P('section', 'tensor'), may hold values from -0.875 to 0.875
- w_up: bfloat16 [2, 768, 3072], P('section', None, 'tensor'), may hold values from -0.21875 to 0.21875
- up_bias: bfloat16 [2, 3072], P('section', 'tensor'), may hold values from -1.5 to 1.5
- w_down: bfloat16 [2, 3072, 768], P('section', 'tensor'), may hold values from -0.109375 to 0.109375
Outputs:
- activations: bfloat16 [2, 16, 1024, 768], P('section', 'dp', 'tensor')
- input_grads: bfloat16 [2, 16, 1024, 768], P('section', 'dp', 'tensor')
- grad_qkv: float32 [2, 768, 3, 768], P('section', None, None, 'tensor')
- grad_qv_bias: float32 [2, 2, 768], P('section', None, 'tensor')
- grad_out: float32 [2, 768, 768], P('section', 'tensor')
- grad_up: float32 [2, 768, 3072], P('section', None, 'tensor')
- grad_up_bias: float32 [2, 3072], P('section', 'tensor')
- grad_down: float32 [2, 3072, 768], P('section', 'tensor')
- grad_gains: float32 [2, 2, 768], P('section')
- grad_shifts: float32 [2, 4, 768], P('section')
Inputs may be any that keep to these rules, and one draw needn't show every extreme that they name: `segments`: each row's numbers never fall; a number's run is 1 to 768 tokens long, and one run of every row has exactly that length.
All inputs are finite; a program needn't handle non-finite values.
Results may differ from a plain program's by a relative error of at most 0.03.
Values may be sent and summed in bfloat16 or wider, within the bound.
A program may use at most 320 MiB of HBM per device.

v0:
```python
import jax
import jax.numpy as jnp
from jax import lax
from jax.sharding import PartitionSpec as P

HEAD = 64
eps_norm = 1e-05


def shifted(block, axis, distance):
    devices = range(lax.axis_size(axis))
    route = [(i - distance, i) for i in devices if i - distance in devices]
    return lax.ppermute(block, axis, route)


def smooth(values_in):
    return jax.nn.gelu(values_in, approximate=True)


def dot_rows(left, right):
    return lax.dot_general(
        left, right, (((0,), (0,)), ((), ())), preferred_element_type=jnp.float32
    )


def dot_last(left, right):
    return lax.dot_general(
        left, right, (((1,), (1,)), ((), ())), preferred_element_type=jnp.float32
    )


def norm_forward(rows_in, gain, shift):
    row_mean = jnp.mean(rows_in, axis=-1, keepdims=True)
    centred = rows_in - row_mean
    inv_dev = lax.rsqrt(jnp.mean(centred * centred, axis=-1, keepdims=True) + eps_norm)
    unit_rows = centred * inv_dev
    return (unit_rows * gain + shift, unit_rows, inv_dev)


def norm_backward(grad_out, unit_rows, inv_dev, gain):
    scaled = grad_out * gain
    grad_in = inv_dev * (
        scaled
        - jnp.mean(scaled, axis=-1, keepdims=True)
        - unit_rows * jnp.mean(scaled * unit_rows, axis=-1, keepdims=True)
    )
    return (grad_in, jnp.sum(grad_out * unit_rows, axis=0), jnp.sum(grad_out, axis=0))


def block_shape(seq_total):
    block_count = max(1, seq_total // 512)
    return (block_count, seq_total // block_count)


def allowed_block(begin_at, block_len, seg_ids):
    q_pos = begin_at + jnp.arange(block_len)
    k_pos = jnp.arange(seg_ids.shape[0])
    q_seg = seg_ids[begin_at : begin_at + block_len]
    return (k_pos[None, :] <= q_pos[:, None]) & (q_seg[:, None] == seg_ids[None, :])


def attention_forward(queries, key_rows, value_rows, seg_ids):
    block_count, block_len = block_shape(queries.shape[0])
    pieces, totals = ([], [])
    for block_no in range(block_count):
        begin_at = block_no * block_len
        scores = jnp.einsum(
            "qhd,khd->hqk",
            queries[begin_at : begin_at + block_len],
            key_rows,
            preferred_element_type=jnp.float32,
        )
        scores = jnp.where(allowed_block(begin_at, block_len, seg_ids)[None], scores, -1e30)
        row_top = jnp.max(scores, axis=-1, keepdims=True)
        weights = jnp.exp(scores - row_top)
        summed = jnp.sum(weights, axis=-1, keepdims=True)
        prob_rows = (weights / summed).astype(jnp.bfloat16)
        pieces.append(
            jnp.einsum("hqk,khd->qhd", prob_rows, value_rows, preferred_element_type=jnp.float32)
        )
        totals.append(row_top + jnp.log(summed))
    return (jnp.concatenate(pieces, axis=0), jnp.concatenate(totals, axis=1))


def attention_backward(queries, key_rows, value_rows, seg_ids, totals, grad_mixed):
    block_count, block_len = block_shape(queries.shape[0])
    grad_queries = []
    grad_keys = jnp.zeros(key_rows.shape, jnp.float32)
    grad_values = jnp.zeros(value_rows.shape, jnp.float32)
    for block_no in range(block_count):
        begin_at = block_no * block_len
        part_query = queries[begin_at : begin_at + block_len]
        part_grad = grad_mixed[begin_at : begin_at + block_len]
        scores = jnp.einsum(
            "qhd,khd->hqk", part_query, key_rows, preferred_element_type=jnp.float32
        )
        scores = jnp.where(allowed_block(begin_at, block_len, seg_ids)[None], scores, -1e30)
        prob_exact = jnp.exp(scores - totals[:, begin_at : begin_at + block_len])
        prob_rows = prob_exact.astype(jnp.bfloat16)
        grad_probs = jnp.einsum(
            "qhd,khd->hqk", part_grad, value_rows, preferred_element_type=jnp.float32
        )
        row_dot = jnp.sum(prob_exact * grad_probs, axis=-1, keepdims=True)
        grad_scores = (prob_exact * (grad_probs - row_dot)).astype(jnp.bfloat16)
        grad_queries.append(
            jnp.einsum("hqk,khd->qhd", grad_scores, key_rows, preferred_element_type=jnp.float32)
        )
        grad_keys = grad_keys + jnp.einsum(
            "hqk,qhd->khd", grad_scores, part_query, preferred_element_type=jnp.float32
        )
        grad_values = grad_values + jnp.einsum(
            "hqk,qhd->khd", prob_rows, part_grad, preferred_element_type=jnp.float32
        )
    return (jnp.concatenate(grad_queries, axis=0), grad_keys, grad_values)


def local(
    inputs,
    segments,
    cotangent,
    norm_gains,
    shared_biases,
    w_qkv,
    qv_bias,
    w_out,
    w_up,
    up_bias,
    w_down,
):
    is_first = lax.axis_index("section") == 0
    micro_count, half_rows, model_width = inputs.shape
    local_width = w_qkv.shape[3]
    head_count = local_width // HEAD
    q_scale = HEAD ** (-0.5)
    gain_rows = norm_gains[0].astype(jnp.float32)
    shifts = shared_biases[0].astype(jnp.float32)
    qkv_mat = w_qkv[0].reshape(model_width, 3 * local_width)
    qv_rows = qv_bias[0].astype(jnp.float32)
    out_mat = w_out[0]
    up_mat, down_mat, up_vec = (w_up[0], w_down[0], up_bias[0])
    up_shift = up_vec.astype(jnp.float32)
    zero_rows = jnp.zeros((half_rows, model_width), jnp.bfloat16)
    received = zero_rows
    outputs, kept_all = ([], [])
    for tick_no in range(micro_count + 1):
        own_micro = min(tick_no, micro_count - 1)
        prior_micro = max(tick_no - 1, 0)
        layer_in = jnp.where(is_first, inputs[own_micro], received).astype(jnp.float32)
        seg_ids = jnp.where(is_first, segments[own_micro], segments[prior_micro])
        normed, forward_unit1, forward_inv1 = norm_forward(layer_in, gain_rows[0], shifts[0])
        forward_normed_all = lax.all_gather(
            normed.astype(jnp.bfloat16), "tensor", axis=0, tiled=True
        )
        forward_seq_total = forward_normed_all.shape[0]
        projected = jnp.dot(
            forward_normed_all, qkv_mat, preferred_element_type=jnp.float32
        ).reshape(forward_seq_total, 3, local_width)
        forward_queries = (
            ((projected[:, 0] + qv_rows[0]) * q_scale)
            .astype(jnp.bfloat16)
            .reshape(forward_seq_total, head_count, HEAD)
        )
        forward_key_rows = (
            projected[:, 1].astype(jnp.bfloat16).reshape(forward_seq_total, head_count, HEAD)
        )
        forward_value_rows = (
            (projected[:, 2] + qv_rows[1])
            .astype(jnp.bfloat16)
            .reshape(forward_seq_total, head_count, HEAD)
        )
        forward_mixed_rows, forward_totals = attention_forward(
            forward_queries, forward_key_rows, forward_value_rows, seg_ids
        )
        forward_mixed_rows = forward_mixed_rows.reshape(forward_seq_total, local_width).astype(
            jnp.bfloat16
        )
        middle = (
            layer_in
            + lax.psum_scatter(
                jnp.dot(forward_mixed_rows, out_mat, preferred_element_type=jnp.float32).astype(
                    jnp.bfloat16
                ),
                "tensor",
                scatter_dimension=0,
                tiled=True,
            ).astype(jnp.float32)
            + shifts[2]
        )
        forward_normed2, forward_unit2, forward_inv2 = norm_forward(middle, gain_rows[1], shifts[1])
        forward_normed2 = forward_normed2.astype(jnp.bfloat16)
        forward_normed2 = lax.all_gather(forward_normed2, "tensor", axis=0, tiled=True)
        forward_hidden = (
            jnp.dot(forward_normed2, up_mat, preferred_element_type=jnp.float32) + up_shift
        )
        forward_active = smooth(forward_hidden).astype(jnp.bfloat16)
        branch2 = lax.psum_scatter(
            jnp.dot(forward_active, down_mat, preferred_element_type=jnp.float32).astype(
                jnp.bfloat16
            ),
            "tensor",
            scatter_dimension=0,
            tiled=True,
        ).astype(jnp.float32)
        output = (middle + branch2 + shifts[3]).astype(jnp.bfloat16)
        forward_kept_state = (
            seg_ids,
            forward_unit1,
            forward_inv1,
            forward_normed_all,
            forward_queries,
            forward_key_rows,
            forward_value_rows,
            forward_totals,
            forward_mixed_rows,
            forward_unit2,
            forward_inv2,
            forward_normed2,
            forward_hidden,
            forward_active,
        )
        output, kept_state = (output, forward_kept_state)
        outputs.append(output)
        kept_all.append(kept_state)
        if tick_no < micro_count:
            received = shifted(output, "section", 1)
    grad_sums = (
        jnp.zeros((model_width, 3 * local_width), jnp.float32),
        jnp.zeros((2, local_width), jnp.float32),
        jnp.zeros(out_mat.shape, jnp.float32),
        jnp.zeros(up_mat.shape, jnp.float32),
        jnp.zeros(up_vec.shape, jnp.float32),
        jnp.zeros(down_mat.shape, jnp.float32),
        jnp.zeros((2, model_width), jnp.float32),
        jnp.zeros((4, model_width), jnp.float32),
    )
    received = zero_rows
    grads_in = []
    for tick_no in range(micro_count + 1):
        kept_slot = micro_count - tick_no
        fresh_grad = cotangent[kept_slot - 1] if kept_slot >= 1 else zero_rows
        incoming = jnp.where(is_first, received, fresh_grad).astype(jnp.float32)
        (
            backward_seg_ids,
            unit1,
            inv1,
            normed_all,
            queries,
            key_rows,
            value_rows,
            totals,
            mixed_rows,
            unit2,
            inv2,
            normed2,
            hidden,
            active,
        ) = kept_all[kept_slot]
        (
            backward_g_qkv,
            backward_g_qv,
            backward_g_out,
            backward_g_up,
            backward_g_upb,
            backward_g_down,
            backward_g_gain,
            backward_g_shift,
        ) = grad_sums
        seq_total = normed_all.shape[0]
        grad_branch2 = incoming.astype(jnp.bfloat16)
        ignored, gelu_back = jax.vjp(smooth, hidden)
        grad_all = lax.all_gather(grad_branch2, "tensor", axis=0, tiled=True)
        grad_active = dot_last(grad_all, down_mat)
        backward_g_down = backward_g_down + dot_rows(active, grad_all)
        grad_hidden = gelu_back(grad_active)[0].astype(jnp.bfloat16)
        backward_g_up = backward_g_up + dot_rows(normed2, grad_hidden)
        backward_g_upb = backward_g_upb + jnp.sum(grad_hidden.astype(jnp.float32), axis=0)
        grad_normed2 = lax.psum_scatter(
            dot_last(grad_hidden, up_mat).astype(jnp.bfloat16),
            "tensor",
            scatter_dimension=0,
            tiled=True,
        ).astype(jnp.float32)
        norm2_grad, gain2, shift2 = norm_backward(grad_normed2, unit2, inv2, gain_rows[1])
        grad_middle = incoming + norm2_grad
        grad_branch = grad_middle.astype(jnp.bfloat16)
        grad_branch_all = lax.all_gather(grad_branch, "tensor", axis=0, tiled=True)
        backward_g_out = backward_g_out + dot_rows(mixed_rows, grad_branch_all)
        grad_mixed = (
            dot_last(grad_branch_all, out_mat)
            .astype(jnp.bfloat16)
            .reshape(seq_total, head_count, HEAD)
        )
        grad_queries, grad_keys, grad_values = attention_backward(
            queries, key_rows, value_rows, backward_seg_ids, totals, grad_mixed
        )
        grad_queries = (grad_queries * q_scale).astype(jnp.bfloat16).reshape(seq_total, local_width)
        grad_keys = grad_keys.astype(jnp.bfloat16).reshape(seq_total, local_width)
        grad_values = grad_values.astype(jnp.bfloat16).reshape(seq_total, local_width)
        grad_proj = jnp.concatenate([grad_queries, grad_keys, grad_values], axis=1)
        backward_g_qkv = backward_g_qkv + dot_rows(normed_all, grad_proj)
        backward_g_qv = backward_g_qv + jnp.stack(
            [
                jnp.sum(grad_queries.astype(jnp.float32), axis=0),
                jnp.sum(grad_values.astype(jnp.float32), axis=0),
            ]
        )
        grad_normed = lax.psum_scatter(
            dot_last(grad_proj, qkv_mat).astype(jnp.bfloat16),
            "tensor",
            scatter_dimension=0,
            tiled=True,
        ).astype(jnp.float32)
        norm1_grad, gain1, shift1 = norm_backward(grad_normed, unit1, inv1, gain_rows[0])
        grad_in = grad_middle + norm1_grad
        backward_g_gain = backward_g_gain + jnp.stack([gain1, gain2])
        backward_g_shift = backward_g_shift + jnp.stack(
            [
                shift1,
                shift2,
                jnp.sum(grad_branch.astype(jnp.float32), axis=0),
                jnp.sum(grad_branch2.astype(jnp.float32), axis=0),
            ]
        )
        grad_in, grad_sums = (
            grad_in.astype(jnp.bfloat16),
            (
                backward_g_qkv,
                backward_g_qv,
                backward_g_out,
                backward_g_up,
                backward_g_upb,
                backward_g_down,
                backward_g_gain,
                backward_g_shift,
            ),
        )
        grads_in.append(grad_in)
        if tick_no < micro_count:
            received = shifted(grad_in, "section", -1)
    act_rows = jnp.stack(
        [
            jnp.where(is_first, outputs[index_no], outputs[index_no + 1])
            for index_no in range(micro_count)
        ]
    )
    grad_rows_out = jnp.stack(
        [
            jnp.where(
                is_first, grads_in[micro_count - index_no], grads_in[micro_count - 1 - index_no]
            )
            for index_no in range(micro_count)
        ]
    )
    g_qkv, g_qv, g_out, g_up, g_upb, g_down, g_gain, g_shift = grad_sums
    g_qkv, g_qv, g_out, g_up, g_upb, g_down = lax.psum(
        (g_qkv, g_qv, g_out, g_up, g_upb, g_down), "dp"
    )
    g_gain, g_shift = lax.psum((g_gain, g_shift), ("tensor", "dp"))
    return (
        act_rows[None],
        grad_rows_out[None],
        g_qkv.reshape(model_width, 3, local_width)[None],
        g_qv[None],
        g_out[None],
        g_up[None],
        g_upb[None],
        g_down[None],
        g_gain[None],
        g_shift[None],
    )


def solution(mesh):
    return jax.shard_map(
        local,
        mesh=mesh,
        in_specs=(
            P("dp", "tensor", None),
            P("dp", None),
            P("dp", "tensor", None),
            P("section", None, None),
            P("section", None, None),
            P("section", None, None, "tensor"),
            P("section", None, "tensor"),
            P("section", "tensor", None),
            P("section", None, "tensor"),
            P("section", "tensor"),
            P("section", "tensor", None),
        ),
        out_specs=(
            P("section", "dp", "tensor", None),
            P("section", "dp", "tensor", None),
            P("section", None, None, "tensor"),
            P("section", None, "tensor"),
            P("section", "tensor", None),
            P("section", None, "tensor"),
            P("section", "tensor"),
            P("section", "tensor", None),
            P("section", None, None),
            P("section", None, None),
        ),
        check_vma=False,
    )
```

profile of v0, /device:TPU:0, one launch (start us, length us, event | category | flops | bytes accessed | tf_op | source)
XLA Modules:
  0.0 1564.0 jit_solution(2588667289465846196)
XLA Ops:
  20.0 24.2 %all-gather.14.cloned.1.call-done = bf16[1024,768]{1,0:T(8,128)(2,1)} async-done(((bf16[512,768]{1,0:T(8,128)(2,1)}), bf16[1024,768]{1,0:T(8,128)(2,1)}) %all-gather.14.cloned.1.call-update) | async-done | bytes 1572880 | tf_op jit(solution)/shard_map/all_gather | solution.py:151
  76.7 26.0 %reduce-scatter.13.cloned.1.call-done = bf16[512,768]{1,0:T(8,128)(2,1)} async-done(((bf16[1024,768]{1,0:T(8,128)(2,1)}), bf16[512,768]{1,0:T(8,128)(2,1)}) %reduce-scatter.13.cloned.1.call-update) | async-done | bytes 786448 | tf_op jit(solution)/shard_map/reduce_scatter | solution.py:179
  108.1 27.3 %all-gather.16.cloned.1.call-done = bf16[1024,768]{1,0:T(8,128)(2,1)} async-done(((bf16[512,768]{1,0:T(8,128)(2,1)}), bf16[1024,768]{1,0:T(8,128)(2,1)}) %all-gather.16.cloned.1.call-update) | async-done | bytes 1572880 | tf_op jit(solution)/shard_map/all_gather | solution.py:191
  147.2 26.2 %reduce-scatter.15.cloned.1.call-done = bf16[512,768]{1,0:T(8,128)(2,1)} async-done(((bf16[1024,768]{1,0:T(8,128)(2,1)}), bf16[512,768]{1,0:T(8,128)(2,1)}) %reduce-scatter.15.cloned.1.call-update) | async-done | bytes 786448 | tf_op jit(solution)/shard_map/reduce_scatter | solution.py:196
  182.9 25.4 %all-gather.18.cloned.1.call-done = bf16[1024,768]{1,0:T(8,128)(2,1)} async-done(((bf16[512,768]{1,0:T(8,128)(2,1)}), bf16[1024,768]{1,0:T(8,128)(2,1)}) %all-gather.18.cloned.1.call-update) | async-done | bytes 1572880 | tf_op jit(solution)/shard_map/all_gather | solution.py:151
  239.0 25.8 %reduce-scatter.17.cloned.1.call-done = bf16[512,768]{1,0:T(8,128)(2,1)} async-done(((bf16[1024,768]{1,0:T(8,128)(2,1)}), bf16[512,768]{1,0:T(8,128)(2,1)}) %reduce-scatter.17.cloned.1.call-update) | async-done | bytes 786448 | tf_op jit(solution)/shard_map/reduce_scatter | solution.py:179
  269.4 27.3 %all-gather.20.cloned.1.call-done = bf16[1024,768]{1,0:T(8,128)(2,1)} async-done(((bf16[512,768]{1,0:T(8,128)(2,1)}), bf16[1024,768]{1,0:T(8,128)(2,1)}) %all-gather.20.cloned.1.call-update) | async-done | bytes 1572880 | tf_op jit(solution)/shard_map/all_gather | solution.py:191
  309.0 26.2 %reduce-scatter.19.cloned.1.call-done = bf16[512,768]{1,0:T(8,128)(2,1)} async-done(((bf16[1024,768]{1,0:T(8,128)(2,1)}), bf16[512,768]{1,0:T(8,128)(2,1)}) %reduce-scatter.19.cloned.1.call-update) | async-done | bytes 786448 | tf_op jit(solution)/shard_map/reduce_scatter | solution.py:196
  345.9 25.4 %all-gather.22.cloned.1.call-done = bf16[1024,768]{1,0:T(8,128)(2,1)} async-done(((bf16[512,768]{1,0:T(8,128)(2,1)}), bf16[1024,768]{1,0:T(8,128)(2,1)}) %all-gather.22.cloned.1.call-update) | async-done | bytes 1572880 | tf_op jit(solution)/shard_map/all_gather | solution.py:151
  402.3 26.0 %reduce-scatter.21.cloned.1.call-done = bf16[512,768]{1,0:T(8,128)(2,1)} async-done(((bf16[1024,768]{1,0:T(8,128)(2,1)}), bf16[512,768]{1,0:T(8,128)(2,1)}) %reduce-scatter.21.cloned.1.call-update) | async-done | bytes 786448 | tf_op jit(solution)/shard_map/reduce_scatter | solution.py:179
  436.3 24.5 %all-gather.24.cloned.1.call-done = bf16[1024,768]{1,0:T(8,128)(2,1)} async-done(((bf16[512,768]{1,0:T(8,128)(2,1)}), bf16[1024,768]{1,0:T(8,128)(2,1)}) %all-gather.24.cloned.1.call-update) | async-done | bytes 1572880 | tf_op jit(solution)/shard_map/all_gather | solution.py:191
  466.7 23.4 %all-gather.36.cloned.1.call-done = bf16[1,1024,768]{2,1,0:T(8,128)(2,1)} async-done(((bf16[1,512,768]{2,1,0:T(8,128)(2,1)}), bf16[1,1024,768]{2,1,0:T(8,128)(2,1)}) %all-gather.36.cloned.1.call-update) | async-done | bytes 1572880 | tf_op jit(solution)/shard_map/all_gather | solution.py:271
  505.0 26.2 %reduce-scatter.25.cloned.1.call-done = bf16[512,768]{1,0:T(8,128)(2,1)} async-done(((bf16[1024,768]{1,0:T(8,128)(2,1)}), bf16[512,768]{1,0:T(8,128)(2,1)}) %reduce-scatter.25.cloned.1.call-update) | async-done | bytes 786448 | tf_op jit(solution)/shard_map/reduce_scatter | solution.py:277
  540.6 24.6 %all-gather.26.cloned.1.call-done = bf16[1024,768]{1,0:T(8,128)(2,1)} async-done(((bf16[512,768]{1,0:T(8,128)(2,1)}), bf16[1024,768]{1,0:T(8,128)(2,1)}) %all-gather.26.cloned.1.call-update) | async-done | bytes 1572880 | tf_op jit(solution)/shard_map/all_gather | solution.py:286
  568.5 11.5 multiply_reduce_fusion.5
  611.8 10.1 multiply_convert_fusion.4
  630.4 26.2 %reduce-scatter.27.cloned.1.call-done = bf16[512,768]{1,0:T(8,128)(2,1)} async-done(((bf16[1024,768]{1,0:T(8,128)(2,1)}), bf16[512,768]{1,0:T(8,128)(2,1)}) %reduce-scatter.27.cloned.1.call-update) | async-done | bytes 786448 | tf_op jit(solution)/shard_map/reduce_scatter | solution.py:307
  668.1 27.3 %all-gather.28.cloned.1.call-done = bf16[1024,768]{1,0:T(8,128)(2,1)} async-done(((bf16[512,768]{1,0:T(8,128)(2,1)}), bf16[1024,768]{1,0:T(8,128)(2,1)}) %all-gather.28.cloned.1.call-update) | async-done | bytes 1572880 | tf_op jit(solution)/shard_map/all_gather | solution.py:271
  710.5 26.0 %reduce-scatter.29.cloned.1.call-done = bf16[512,768]{1,0:T(8,128)(2,1)} async-done(((bf16[1024,768]{1,0:T(8,128)(2,1)}), bf16[512,768]{1,0:T(8,128)(2,1)}) %reduce-scatter.29.cloned.1.call-update) | async-done | bytes 786448 | tf_op jit(solution)/shard_map/reduce_scatter | solution.py:277
  743.8 26.1 %all-gather.30.cloned.1.call-done = bf16[1024,768]{1,0:T(8,128)(2,1)} async-done(((bf16[512,768]{1,0:T(8,128)(2,1)}), bf16[1024,768]{1,0:T(8,128)(2,1)}) %all-gather.30.cloned.1.call-update) | async-done | bytes 1572880 | tf_op jit(solution)/shard_map/all_gather | solution.py:286
  773.2 11.2 multiply_reduce_fusion.3
  816.3 10.0 multiply_convert_fusion.2
  834.8 26.2 %reduce-scatter.31.cloned.1.call-done = bf16[512,768]{1,0:T(8,128)(2,1)} async-done(((bf16[1024,768]{1,0:T(8,128)(2,1)}), bf16[512,768]{1,0:T(8,128)(2,1)}) %reduce-scatter.31.cloned.1.call-update) | async-done | bytes 786448 | tf_op jit(solution)/shard_map/reduce_scatter | solution.py:307
  873.4 27.3 %all-gather.32.cloned.1.call-done = bf16[1024,768]{1,0:T(8,128)(2,1)} async-done(((bf16[512,768]{1,0:T(8,128)(2,1)}), bf16[1024,768]{1,0:T(8,128)(2,1)}) %all-gather.32.cloned.1.call-update) | async-done | bytes 1572880 | tf_op jit(solution)/shard_map/all_gather | solution.py:271
  916.4 25.4 %reduce-scatter.33.cloned.1.call-done = bf16[512,768]{1,0:T(8,128)(2,1)} async-done(((bf16[1024,768]{1,0:T(8,128)(2,1)}), bf16[512,768]{1,0:T(8,128)(2,1)}) %reduce-scatter.33.cloned.1.call-update) | async-done | bytes 786448 | tf_op jit(solution)/shard_map/reduce_scatter | solution.py:277
  999.0 11.6 multiply_reduce_fusion.1
  1029.7 12.2 multiply_convert_fusion
  1065.7 10.2 add_bitcast_fusion.1
  1075.9 12.0 add_bitcast_fusion
  1106.1 23.8 %all-reduce.1 = (f32[1,2,384]{2,1,0:T(2,128)}, f32[1,1536]{1,0:T(1,128)}) all-reduce(f32[1,2,384]{2,1,0:T(2,128)S(1)} %fusion.263, f32[1,1536]{1,0:T(1,128)S(1)} %broadcast_in_dim.102), channel_id=1, replica_groups=mesh['section'=2,'tensor'=2,'dp'=8] {'dp'}, use_global_device_ids=true, to_apply=%region_61.62 | all-reduce | flops 2304 | bytes 18432 | tf_op jit(solution)/shard_map/psum | solution.py:355
  1132.2 76.4 %all-reduce = (f32[1,2,768]{2,1,0:T(2,128)}, f32[1,4,768]{2,1,0:T(4,128)}) all-reduce(f32[1,2,768]{2,1,0:T(2,128)S(1)} %fusion.261, f32[1,4,768]{2,1,0:T(4,128)S(1)} %fusion.259), channel_id=1, replica_groups=mesh['section'=2,'tensor'=2,'dp'=8] {'tensor','dp'}, use_global_device_ids=true, to_apply=%region_75.76 | all-reduce | flops 4608 | bytes 36864 | tf_op jit(solution)/shard_map/psum | solution.py:358
  1212.6 330.6 %all-reduce.5.cloned.1.call-done = (f32[1,768,3,384]{1,3,2,0:T(8,128)}, f32[1,384,768]{2,1,0:T(8,128)}, f32[1,768,1536]{2,1,0:T(8,128)}, f32[1,1536,768]{2,1,0:T(8,128)}) async-done(((f32[1,768,3,384]{1,3,2,0:T(8,128)}, f32[1,384,768]{2,1,0:T(8,128)}, f32[1,768,1536]{2,1,0:T(8,128)}, f32[1,1536,768]{2,1,0:T(8,128)}), (f32[1,768,3,384]{1,3,2,0:T(8,128)}, f32[1,384,768]{2,1,0:T(8,128)}, ...) | async-done | bytes 14155792 | tf_op jit(solution)/shard_map/psum | solution.py:355
  (775 shorter events, 484.2 us)
Async XLA Ops:
  7.2 37.1 %all-gather.14.cloned.1.call-start = ((), (), s32[]{:S(2)}) async-start(), calls=%async_computation.12 | async-start | bytes 2359296 | tf_op jit(solution)/shard_map/all_gather | solution.py:151
  11.8 852.0 %copy-start.110 = (f32[768]{0:T(1024)}, f32[768]{0:T(1024)S(1)}, u32[]{:S(2)}) copy-start(f32[768]{0:T(1024)S(1)} %get-tuple-element.155) | copy-start | bytes 9220
  14.2 88.5 %reduce-scatter.13.cloned.1.call-start = ((), (), s32[]{:S(2)}) async-start(), calls=%async_computation.13 | async-start | bytes 2359296 | tf_op jit(solution)/shard_map/reduce_scatter | solution.py:179
  14.3 198.2 %copy-start.180 = (f32[384]{0:T(512)}, f32[384]{0:T(512)S(1)}, u32[]{:S(2)}) copy-start(f32[384]{0:T(512)S(1)} %get-tuple-element.50) | copy-start | bytes 4612
  76.5 58.9 %all-gather.16.cloned.1.call-start = ((), (), s32[]{:S(2)}) async-start(), calls=%async_computation.14 | async-start | bytes 2359296 | tf_op jit(solution)/shard_map/all_gather | solution.py:191
  108.0 65.3 %reduce-scatter.15.cloned.1.call-start = ((), (), s32[]{:S(2)}) async-start(), calls=%async_computation.15 | async-start | bytes 2359296 | tf_op jit(solution)/shard_map/reduce_scatter | solution.py:196
  147.1 61.2 %all-gather.18.cloned.1.call-start = ((), (), s32[]{:S(2)}) async-start(), calls=%async_computation.16 | async-start | bytes 2359296 | tf_op jit(solution)/shard_map/all_gather | solution.py:151
  175.3 3.6 collective-permute-start
  180.9 83.9 %reduce-scatter.17.cloned.1.call-start = ((), (), s32[]{:S(2)}) async-start(), calls=%async_computation.17 | async-start | bytes 2359296 | tf_op jit(solution)/shard_map/reduce_scatter | solution.py:179
  238.6 58.2 %all-gather.20.cloned.1.call-start = ((), (), s32[]{:S(2)}) async-start(), calls=%async_computation.18 | async-start | bytes 2359296 | tf_op jit(solution)/shard_map/all_gather | solution.py:191
  269.4 65.8 %reduce-scatter.19.cloned.1.call-start = ((), (), s32[]{:S(2)}) async-start(), calls=%async_computation.19 | async-start | bytes 2359296 | tf_op jit(solution)/shard_map/reduce_scatter | solution.py:196
  309.0 62.4 %all-gather.22.cloned.1.call-start = ((), (), s32[]{:S(2)}) async-start(), calls=%async_computation.20 | async-start | bytes 2359296 | tf_op jit(solution)/shard_map/all_gather | solution.py:151
  338.4 3.5 collective-permute-start.1
  342.3 317.0 %copy-start.7 = (bf16[512,768]{1,0:T(8,128)(2,1)}, bf16[512,768]{1,0:T(8,128)(2,1)S(1)}, u32[]{:S(2)}) copy-start(bf16[512,768]{1,0:T(8,128)(2,1)S(1)} %get-tuple-element.86) | copy-start | bytes 2359300
  344.0 84.4 %reduce-scatter.21.cloned.1.call-start = ((), (), s32[]{:S(2)}) async-start(), calls=%async_computation.21 | async-start | bytes 2359296 | tf_op jit(solution)/shard_map/reduce_scatter | solution.py:179
  402.1 58.7 %all-gather.24.cloned.1.call-start = ((), (), s32[]{:S(2)}) async-start(), calls=%async_computation.22 | async-start | bytes 2359296 | tf_op jit(solution)/shard_map/all_gather | solution.py:191
  433.4 56.7 %all-gather.36.cloned.1.call-start = ((), (), s32[]{:S(2)}) async-start(), calls=%async_computation.35 | async-start | bytes 2359296 | tf_op jit(solution)/shard_map/all_gather | solution.py:271
  436.3 94.9 %reduce-scatter.25.cloned.1.call-start = ((), (), s32[]{:S(2)}) async-start(), calls=%async_computation.24 | async-start | bytes 2359296 | tf_op jit(solution)/shard_map/reduce_scatter | solution.py:277
  505.0 60.3 %all-gather.26.cloned.1.call-start = ((), (), s32[]{:S(2)}) async-start(), calls=%async_computation.25 | async-start | bytes 2359296 | tf_op jit(solution)/shard_map/all_gather | solution.py:286
  537.9 118.7 %reduce-scatter.27.cloned.1.call-start = ((), (), s32[]{:S(2)}) async-start(), calls=%async_computation.26 | async-start | bytes 2359296 | tf_op jit(solution)/shard_map/reduce_scatter | solution.py:307
  630.3 65.1 %all-gather.28.cloned.1.call-start = ((), (), s32[]{:S(2)}) async-start(), calls=%async_computation.27 | async-start | bytes 2359296 | tf_op jit(solution)/shard_map/all_gather | solution.py:271
  662.0 4.3 collective-permute-start.2
  668.1 68.4 %reduce-scatter.29.cloned.1.call-start = ((), (), s32[]{:S(2)}) async-start(), calls=%async_computation.28 | async-start | bytes 2359296 | tf_op jit(solution)/shard_map/reduce_scatter | solution.py:277
  710.3 59.6 %all-gather.30.cloned.1.call-start = ((), (), s32[]{:S(2)}) async-start(), calls=%async_computation.29 | async-start | bytes 2359296 | tf_op jit(solution)/shard_map/all_gather | solution.py:286
  742.5 118.5 %reduce-scatter.31.cloned.1.call-start = ((), (), s32[]{:S(2)}) async-start(), calls=%async_computation.30 | async-start | bytes 2359296 | tf_op jit(solution)/shard_map/reduce_scatter | solution.py:307
  834.8 65.9 %all-gather.32.cloned.1.call-start = ((), (), s32[]{:S(2)}) async-start(), calls=%async_computation.31 | async-start | bytes 2359296 | tf_op jit(solution)/shard_map/all_gather | solution.py:271
  867.5 4.2 collective-permute-start.3
  873.3 68.5 %reduce-scatter.33.cloned.1.call-start = ((), (), s32[]{:S(2)}) async-start(), calls=%async_computation.32 | async-start | bytes 2359296 | tf_op jit(solution)/shard_map/reduce_scatter | solution.py:277
  915.5 80.9 %all-gather.34.cloned.1.call-start = ((), (), s32[]{:S(2)}) async-start(), calls=%async_computation.33 | async-start | bytes 2359296 | tf_op jit(solution)/shard_map/all_gather | solution.py:286
  949.1 152.4 %reduce-scatter.23.cloned.1.call-start = ((), (), s32[]{:S(2)}) async-start(), calls=%async_computation.23 | async-start | bytes 2359296 | tf_op jit(solution)/shard_map/reduce_scatter | solution.py:196
  962.9 166.9 %reduce-scatter.35.cloned.1.call-start = ((), (), s32[]{:S(2)}) async-start(), calls=%async_computation.34 | async-start | bytes 2359296 | tf_op jit(solution)/shard_map/reduce_scatter | solution.py:307
  1065.6 477.7 %all-reduce.5.cloned.1.call-start = ((), (), s32[]{:S(2)}) async-start(), calls=%async_computation.36 | async-start | bytes 28311552 | tf_op jit(solution)/shard_map/psum | solution.py:355
  (243 other events, 3039.0 us)
Sparse Core Ops, SparseCore 0:
  14.3 29.8 all-gather.13
  76.6 26.0 reduce-scatter.12
  108.1 27.2 all-gather.15
  147.2 26.0 reduce-scatter.14
  181.1 27.2 all-gather.17
  238.7 26.0 reduce-scatter.16
  269.5 27.2 all-gather.19
  309.1 26.0 reduce-scatter.18
  344.1 27.2 all-gather.21
  402.2 26.0 reduce-scatter.20
  433.6 27.2 all-gather.23
  462.8 27.1 all-gather.35
  505.1 26.0 reduce-scatter.24
  538.0 27.2 all-gather.25
  630.4 26.0 reduce-scatter.26
  668.2 27.2 all-gather.27
  710.4 26.0 reduce-scatter.28
  742.6 27.2 all-gather.29
  834.9 26.0 reduce-scatter.30
  873.4 27.2 all-gather.31
  915.7 26.0 reduce-scatter.32
  949.2 27.2 all-gather.33
  979.2 26.0 reduce-scatter.22
  1065.7 26.1 reduce-scatter.34
  1100.8 442.3 all-reduce.4
where the time goes:
time: 1570 us; the launch traced here: 1560 us
  waiting for transfers between devices  883 us (56%)
  matrix products  325 us (21%)
  other arithmetic  167 us (11%)
  blocking collectives  100 us (6%)
  local copies, waits for them, and re-layouts  62.7 us (4%)
  between operations  17.2 us (1%)
    psum x1, waiting for transfers between devices, local(): lax.psum((g_qkv, g_qv, g_out, g_up, g_upb, g_down), 'dp')  331 us
    all_gather x3, waiting for transfers between devices, local(): lax.all_gather(forward_normed2, 'tensor', axis=0, tiled=True)  79 us
    all_gather x3, waiting for transfers between devices, local(): grad_all = lax.all_gather(grad_branch2, 'tensor', axis=0, tiled=True)  78 us
    reduce_scatter x3, waiting for transfers between devices, local(): lax.psum_scatter(jnp.dot(forward_mixed_rows, out_mat, preferred_element_t...  77.8 us
    reduce_scatter x3, waiting for transfers between devices, local(): lax.psum_scatter(dot_last(grad_hidden, up_mat).astype(jnp.bfloat16), 'ten...  77.6 us
    psum x1, blocking collectives, local(): g_gain, g_shift = lax.psum((g_gain, g_shift), ('tensor', 'dp'))  76.4 us
    all_gather x3, waiting for transfers between devices, local(): lax.all_gather(normed.astype(jnp.bfloat16), 'tensor', axis=0, tiled=True)  75.1 us
    dot_general x6, matrix products, attention_backward(): jnp.einsum('qhd,khd->hqk', part_grad, value_rows, preferred_element_type=...  63 us
  transfers between devices with their start and end apart: 29, of which 26 were waited for; matrix products, arithmetic and copies ran while one was open for 11% of the time, Pallas kernels for 0%

commit v1 on v0

--- a/solution.py
+++ b/solution.py
@@ -355,7 +355,7 @@
     g_qkv, g_qv, g_out, g_up, g_upb, g_down = lax.psum(
         (g_qkv, g_qv, g_out, g_up, g_upb, g_down), "dp"
     )
-    g_gain, g_shift = lax.psum((g_gain, g_shift), ("tensor", "dp"))
+    g_gain, g_shift = lax.psum(lax.psum((g_gain, g_shift), "dp"), "tensor")
     return (
         act_rows[None],
         grad_rows_out[None],

time: 1570 us -> 1570 us (level)
  blocking collectives: 100 us -> 47 us
  waiting for transfers between devices: 883 us -> 935 us
    psum x1, blocking collectives: 76.4 us -> 7.39 us  [local(): g_gain, g_shift = lax.psum(lax.psum((g_gain, g_shift), 'dp'), 'tensor')]
    psum x1, waiting for transfers between devices: 331 us -> 382 us  [local(): lax.psum((g_qkv, g_qv, g_out, g_up, g_upb, g_down), 'dp')]
    psum x1, blocking collectives: 23.8 us -> 39.6 us  [local(): lax.psum((g_qkv, g_qv, g_out, g_up, g_upb, g_down), 'dp')]
  transfers between devices with their start and end apart: 29 -> 29, of which waited for: 26 -> 26; matrix products, arithmetic and copies ran while one was open for 11% -> 12% of each run, Pallas kernels for 0% -> 0%
where the time goes in v1:
time: 1570 us; the launch traced here: 1560 us
  waiting for transfers between devices  935 us (60%)
  matrix products  325 us (21%)
  other arithmetic  168 us (11%)
  local copies, waits for them, and re-layouts  62.7 us (4%)
  blocking collectives  47 us (3%)
  between operations  17.2 us (1%)
    psum x1, waiting for transfers between devices, local(): lax.psum((g_qkv, g_qv, g_out, g_up, g_upb, g_down), 'dp')  382 us
    all_gather x3, waiting for transfers between devices, local(): lax.all_gather(forward_normed2, 'tensor', axis=0, tiled=True)  79 us
    all_gather x3, waiting for transfers between devices, local(): grad_all = lax.all_gather(grad_branch2, 'tensor', axis=0, tiled=True)  78 us
    reduce_scatter x3, waiting for transfers between devices, local(): lax.psum_scatter(jnp.dot(forward_mixed_rows, out_mat, preferred_element_t...  77.8 us
    reduce_scatter x3, waiting for transfers between devices, local(): lax.psum_scatter(dot_last(grad_hidden, up_mat).astype(jnp.bfloat16), 'ten...  77.6 us
    all_gather x3, waiting for transfers between devices, local(): lax.all_gather(normed.astype(jnp.bfloat16), 'tensor', axis=0, tiled=True)  75.1 us
    dot_general x6, matrix products, attention_backward(): jnp.einsum('qhd,khd->hqk', part_grad, value_rows, preferred_element_type=...  63 us
    dot_general x12, matrix products, dot_rows(): lax.dot_general(left, right, (((0,), (0,)), ((), ())), preferred_element_...  61.3 us
  transfers between devices with their start and end apart: 29, of which 26 were waited for; matrix products, arithmetic and copies ran while one was open for 12% of the time, Pallas kernels for 0%

profile of v1, /device:TPU:0, one launch (start us, length us, event | category | flops | bytes accessed | tf_op | source)
XLA Modules:
  0.0 1562.3 jit_solution(8378889533231111412)
XLA Ops:
  20.0 24.2 %all-gather.14.cloned.1.call-done = bf16[1024,768]{1,0:T(8,128)(2,1)} async-done(((bf16[512,768]{1,0:T(8,128)(2,1)}), bf16[1024,768]{1,0:T(8,128)(2,1)}) %all-gather.14.cloned.1.call-update) | async-done | bytes 1572880 | tf_op jit(solution)/shard_map/all_gather | solution.py:151
  76.7 26.0 %reduce-scatter.13.cloned.1.call-done = bf16[512,768]{1,0:T(8,128)(2,1)} async-done(((bf16[1024,768]{1,0:T(8,128)(2,1)}), bf16[512,768]{1,0:T(8,128)(2,1)}) %reduce-scatter.13.cloned.1.call-update) | async-done | bytes 786448 | tf_op jit(solution)/shard_map/reduce_scatter | solution.py:179
  108.1 27.3 %all-gather.16.cloned.1.call-done = bf16[1024,768]{1,0:T(8,128)(2,1)} async-done(((bf16[512,768]{1,0:T(8,128)(2,1)}), bf16[1024,768]{1,0:T(8,128)(2,1)}) %all-gather.16.cloned.1.call-update) | async-done | bytes 1572880 | tf_op jit(solution)/shard_map/all_gather | solution.py:191
  147.2 26.2 %reduce-scatter.15.cloned.1.call-done = bf16[512,768]{1,0:T(8,128)(2,1)} async-done(((bf16[1024,768]{1,0:T(8,128)(2,1)}), bf16[512,768]{1,0:T(8,128)(2,1)}) %reduce-scatter.15.cloned.1.call-update) | async-done | bytes 786448 | tf_op jit(solution)/shard_map/reduce_scatter | solution.py:196
  182.9 25.4 %all-gather.18.cloned.1.call-done = bf16[1024,768]{1,0:T(8,128)(2,1)} async-done(((bf16[512,768]{1,0:T(8,128)(2,1)}), bf16[1024,768]{1,0:T(8,128)(2,1)}) %all-gather.18.cloned.1.call-update) | async-done | bytes 1572880 | tf_op jit(solution)/shard_map/all_gather | solution.py:151
  239.0 25.8 %reduce-scatter.17.cloned.1.call-done = bf16[512,768]{1,0:T(8,128)(2,1)} async-done(((bf16[1024,768]{1,0:T(8,128)(2,1)}), bf16[512,768]{1,0:T(8,128)(2,1)}) %reduce-scatter.17.cloned.1.call-update) | async-done | bytes 786448 | tf_op jit(solution)/shard_map/reduce_scatter | solution.py:179
  269.4 27.3 %all-gather.20.cloned.1.call-done = bf16[1024,768]{1,0:T(8,128)(2,1)} async-done(((bf16[512,768]{1,0:T(8,128)(2,1)}), bf16[1024,768]{1,0:T(8,128)(2,1)}) %all-gather.20.cloned.1.call-update) | async-done | bytes 1572880 | tf_op jit(solution)/shard_map/all_gather | solution.py:191
  309.0 26.2 %reduce-scatter.19.cloned.1.call-done = bf16[512,768]{1,0:T(8,128)(2,1)} async-done(((bf16[1024,768]{1,0:T(8,128)(2,1)}), bf16[512,768]{1,0:T(8,128)(2,1)}) %reduce-scatter.19.cloned.1.call-update) | async-done | bytes 786448 | tf_op jit(solution)/shard_map/reduce_scatter | solution.py:196
  345.9 25.4 %all-gather.22.cloned.1.call-done = bf16[1024,768]{1,0:T(8,128)(2,1)} async-done(((bf16[512,768]{1,0:T(8,128)(2,1)}), bf16[1024,768]{1,0:T(8,128)(2,1)}) %all-gather.22.cloned.1.call-update) | async-done | bytes 1572880 | tf_op jit(solution)/shard_map/all_gather | solution.py:151
  402.3 26.0 %reduce-scatter.21.cloned.1.call-done = bf16[512,768]{1,0:T(8,128)(2,1)} async-done(((bf16[1024,768]{1,0:T(8,128)(2,1)}), bf16[512,768]{1,0:T(8,128)(2,1)}) %reduce-scatter.21.cloned.1.call-update) | async-done | bytes 786448 | tf_op jit(solution)/shard_map/reduce_scatter | solution.py:179
  436.3 24.5 %all-gather.24.cloned.1.call-done = bf16[1024,768]{1,0:T(8,128)(2,1)} async-done(((bf16[512,768]{1,0:T(8,128)(2,1)}), bf16[1024,768]{1,0:T(8,128)(2,1)}) %all-gather.24.cloned.1.call-update) | async-done | bytes 1572880 | tf_op jit(solution)/shard_map/all_gather | solution.py:191
  466.7 23.4 %all-gather.36.cloned.1.call-done = bf16[1,1024,768]{2,1,0:T(8,128)(2,1)} async-done(((bf16[1,512,768]{2,1,0:T(8,128)(2,1)}), bf16[1,1024,768]{2,1,0:T(8,128)(2,1)}) %all-gather.36.cloned.1.call-update) | async-done | bytes 1572880 | tf_op jit(solution)/shard_map/all_gather | solution.py:271
  505.0 26.2 %reduce-scatter.25.cloned.1.call-done = bf16[512,768]{1,0:T(8,128)(2,1)} async-done(((bf16[1024,768]{1,0:T(8,128)(2,1)}), bf16[512,768]{1,0:T(8,128)(2,1)}) %reduce-scatter.25.cloned.1.call-update) | async-done | bytes 786448 | tf_op jit(solution)/shard_map/reduce_scatter | solution.py:277
  540.6 24.6 %all-gather.26.cloned.1.call-done = bf16[1024,768]{1,0:T(8,128)(2,1)} async-done(((bf16[512,768]{1,0:T(8,128)(2,1)}), bf16[1024,768]{1,0:T(8,128)(2,1)}) %all-gather.26.cloned.1.call-update) | async-done | bytes 1572880 | tf_op jit(solution)/shard_map/all_gather | solution.py:286
  568.5 11.5 multiply_reduce_fusion.5
  598.5 9.6 multiply_reduce_fusion.4
  611.8 10.1 multiply_convert_fusion.4
  630.4 26.2 %reduce-scatter.27.cloned.1.call-done = bf16[512,768]{1,0:T(8,128)(2,1)} async-done(((bf16[1024,768]{1,0:T(8,128)(2,1)}), bf16[512,768]{1,0:T(8,128)(2,1)}) %reduce-scatter.27.cloned.1.call-update) | async-done | bytes 786448 | tf_op jit(solution)/shard_map/reduce_scatter | solution.py:307
  668.1 27.3 %all-gather.28.cloned.1.call-done = bf16[1024,768]{1,0:T(8,128)(2,1)} async-done(((bf16[512,768]{1,0:T(8,128)(2,1)}), bf16[1024,768]{1,0:T(8,128)(2,1)}) %all-gather.28.cloned.1.call-update) | async-done | bytes 1572880 | tf_op jit(solution)/shard_map/all_gather | solution.py:271
  710.5 26.0 %reduce-scatter.29.cloned.1.call-done = bf16[512,768]{1,0:T(8,128)(2,1)} async-done(((bf16[1024,768]{1,0:T(8,128)(2,1)}), bf16[512,768]{1,0:T(8,128)(2,1)}) %reduce-scatter.29.cloned.1.call-update) | async-done | bytes 786448 | tf_op jit(solution)/shard_map/reduce_scatter | solution.py:277
  743.8 26.1 %all-gather.30.cloned.1.call-done = bf16[1024,768]{1,0:T(8,128)(2,1)} async-done(((bf16[512,768]{1,0:T(8,128)(2,1)}), bf16[1024,768]{1,0:T(8,128)(2,1)}) %all-gather.30.cloned.1.call-update) | async-done | bytes 1572880 | tf_op jit(solution)/shard_map/all_gather | solution.py:286
  773.2 11.2 multiply_reduce_fusion.3
  816.3 10.0 multiply_convert_fusion.2
  834.8 26.2 %reduce-scatter.31.cloned.1.call-done = bf16[512,768]{1,0:T(8,128)(2,1)} async-done(((bf16[1024,768]{1,0:T(8,128)(2,1)}), bf16[512,768]{1,0:T(8,128)(2,1)}) %reduce-scatter.31.cloned.1.call-update) | async-done | bytes 786448 | tf_op jit(solution)/shard_map/reduce_scatter | solution.py:307
  873.4 27.3 %all-gather.32.cloned.1.call-done = bf16[1024,768]{1,0:T(8,128)(2,1)} async-done(((bf16[512,768]{1,0:T(8,128)(2,1)}), bf16[1024,768]{1,0:T(8,128)(2,1)}) %all-gather.32.cloned.1.call-update) | async-done | bytes 1572880 | tf_op jit(solution)/shard_map/all_gather | solution.py:271
  916.4 25.4 %reduce-scatter.33.cloned.1.call-done = bf16[512,768]{1,0:T(8,128)(2,1)} async-done(((bf16[1024,768]{1,0:T(8,128)(2,1)}), bf16[512,768]{1,0:T(8,128)(2,1)}) %reduce-scatter.33.cloned.1.call-update) | async-done | bytes 786448 | tf_op jit(solution)/shard_map/reduce_scatter | solution.py:277
  999.0 11.6 multiply_reduce_fusion.1
  1029.7 12.2 multiply_convert_fusion
  1065.7 10.2 add_bitcast_fusion.1
  1075.9 12.0 add_bitcast_fusion
  1109.0 39.6 %all-reduce = (f32[1,2,384]{2,1,0:T(2,128)}, f32[1,1536]{1,0:T(1,128)}, f32[2,768]{1,0:T(2,128)S(1)}, f32[4,768]{1,0:T(4,128)S(1)}) all-reduce(f32[1,2,384]{2,1,0:T(2,128)S(1)} %fusion.261, f32[1,1536]{1,0:T(1,128)S(1)} %broadcast_in_dim.102, f32[2,768]{1,0:T(2,128)S(1)} %fusion.259, ...), channel_id=1, replica_groups=mesh['section'=2,'tensor'=2,'dp'=8] {'dp'}, use_global_device_ids=true, to_apply=%region_61.62 | all-reduce | flops 6912 | bytes 55296 | tf_op jit(solution)/shard_map/psum | solution.py:355
  1159.9 381.7 %all-reduce.5.cloned.1.call-done = (f32[1,768,3,384]{1,3,2,0:T(8,128)}, f32[1,384,768]{2,1,0:T(8,128)}, f32[1,768,1536]{2,1,0:T(8,128)}, f32[1,1536,768]{2,1,0:T(8,128)}) async-done(((f32[1,768,3,384]{1,3,2,0:T(8,128)}, f32[1,384,768]{2,1,0:T(8,128)}, f32[1,768,1536]{2,1,0:T(8,128)}, f32[1,1536,768]{2,1,0:T(8,128)}), (f32[1,768,3,384]{1,3,2,0:T(8,128)}, f32[1,384,768]{2,1,0:T(8,128)}, ...) | async-done | bytes 14155792 | tf_op jit(solution)/shard_map/psum | solution.py:355
  (775 shorter events, 482.5 us)
Async XLA Ops:
  7.2 37.1 %all-gather.14.cloned.1.call-start = ((), (), s32[]{:S(2)}) async-start(), calls=%async_computation.12 | async-start | bytes 2359296 | tf_op jit(solution)/shard_map/all_gather | solution.py:151
  11.8 852.0 %copy-start.110 = (f32[768]{0:T(1024)}, f32[768]{0:T(1024)S(1)}, u32[]{:S(2)}) copy-start(f32[768]{0:T(1024)S(1)} %get-tuple-element.157) | copy-start | bytes 9220
  14.2 88.5 %reduce-scatter.13.cloned.1.call-start = ((), (), s32[]{:S(2)}) async-start(), calls=%async_computation.13 | async-start | bytes 2359296 | tf_op jit(solution)/shard_map/reduce_scatter | solution.py:179
  14.3 198.2 %copy-start.180 = (f32[384]{0:T(512)}, f32[384]{0:T(512)S(1)}, u32[]{:S(2)}) copy-start(f32[384]{0:T(512)S(1)} %get-tuple-element.50) | copy-start | bytes 4612
  76.5 58.9 %all-gather.16.cloned.1.call-start = ((), (), s32[]{:S(2)}) async-start(), calls=%async_computation.14 | async-start | bytes 2359296 | tf_op jit(solution)/shard_map/all_gather | solution.py:191
  108.0 65.3 %reduce-scatter.15.cloned.1.call-start = ((), (), s32[]{:S(2)}) async-start(), calls=%async_computation.15 | async-start | bytes 2359296 | tf_op jit(solution)/shard_map/reduce_scatter | solution.py:196
  147.1 61.2 %all-gather.18.cloned.1.call-start = ((), (), s32[]{:S(2)}) async-start(), calls=%async_computation.16 | async-start | bytes 2359296 | tf_op jit(solution)/shard_map/all_gather | solution.py:151
  175.3 3.6 collective-permute-start
  180.9 83.9 %reduce-scatter.17.cloned.1.call-start = ((), (), s32[]{:S(2)}) async-start(), calls=%async_computation.17 | async-start | bytes 2359296 | tf_op jit(solution)/shard_map/reduce_scatter | solution.py:179
  238.6 58.2 %all-gather.20.cloned.1.call-start = ((), (), s32[]{:S(2)}) async-start(), calls=%async_computation.18 | async-start | bytes 2359296 | tf_op jit(solution)/shard_map/all_gather | solution.py:191
  269.4 65.8 %reduce-scatter.19.cloned.1.call-start = ((), (), s32[]{:S(2)}) async-start(), calls=%async_computation.19 | async-start | bytes 2359296 | tf_op jit(solution)/shard_map/reduce_scatter | solution.py:196
  309.0 62.4 %all-gather.22.cloned.1.call-start = ((), (), s32[]{:S(2)}) async-start(), calls=%async_computation.20 | async-start | bytes 2359296 | tf_op jit(solution)/shard_map/all_gather | solution.py:151
  338.4 3.5 collective-permute-start.1
  342.3 317.0 %copy-start.7 = (bf16[512,768]{1,0:T(8,128)(2,1)}, bf16[512,768]{1,0:T(8,128)(2,1)S(1)}, u32[]{:S(2)}) copy-start(bf16[512,768]{1,0:T(8,128)(2,1)S(1)} %get-tuple-element.88) | copy-start | bytes 2359300
  344.0 84.4 %reduce-scatter.21.cloned.1.call-start = ((), (), s32[]{:S(2)}) async-start(), calls=%async_computation.21 | async-start | bytes 2359296 | tf_op jit(solution)/shard_map/reduce_scatter | solution.py:179
  402.1 58.7 %all-gather.24.cloned.1.call-start = ((), (), s32[]{:S(2)}) async-start(), calls=%async_computation.22 | async-start | bytes 2359296 | tf_op jit(solution)/shard_map/all_gather | solution.py:191
  433.4 56.7 %all-gather.36.cloned.1.call-start = ((), (), s32[]{:S(2)}) async-start(), calls=%async_computation.35 | async-start | bytes 2359296 | tf_op jit(solution)/shard_map/all_gather | solution.py:271
  436.3 94.9 %reduce-scatter.25.cloned.1.call-start = ((), (), s32[]{:S(2)}) async-start(), calls=%async_computation.24 | async-start | bytes 2359296 | tf_op jit(solution)/shard_map/reduce_scatter | solution.py:277
  505.0 60.3 %all-gather.26.cloned.1.call-start = ((), (), s32[]{:S(2)}) async-start(), calls=%async_computation.25 | async-start | bytes 2359296 | tf_op jit(solution)/shard_map/all_gather | solution.py:286
  537.9 118.7 %reduce-scatter.27.cloned.1.call-start = ((), (), s32[]{:S(2)}) async-start(), calls=%async_computation.26 | async-start | bytes 2359296 | tf_op jit(solution)/shard_map/reduce_scatter | solution.py:307
  630.3 65.1 %all-gather.28.cloned.1.call-start = ((), (), s32[]{:S(2)}) async-start(), calls=%async_computation.27 | async-start | bytes 2359296 | tf_op jit(solution)/shard_map/all_gather | solution.py:271
  662.0 4.3 collective-permute-start.2
  668.1 68.4 %reduce-scatter.29.cloned.1.call-start = ((), (), s32[]{:S(2)}) async-start(), calls=%async_computation.28 | async-start | bytes 2359296 | tf_op jit(solution)/shard_map/reduce_scatter | solution.py:277
  710.3 59.6 %all-gather.30.cloned.1.call-start = ((), (), s32[]{:S(2)}) async-start(), calls=%async_computation.29 | async-start | bytes 2359296 | tf_op jit(solution)/shard_map/all_gather | solution.py:286
  742.5 118.5 %reduce-scatter.31.cloned.1.call-start = ((), (), s32[]{:S(2)}) async-start(), calls=%async_computation.30 | async-start | bytes 2359296 | tf_op jit(solution)/shard_map/reduce_scatter | solution.py:307
  834.8 65.9 %all-gather.32.cloned.1.call-start = ((), (), s32[]{:S(2)}) async-start(), calls=%async_computation.31 | async-start | bytes 2359296 | tf_op jit(solution)/shard_map/all_gather | solution.py:271
  867.5 4.2 collective-permute-start.3
  873.3 68.5 %reduce-scatter.33.cloned.1.call-start = ((), (), s32[]{:S(2)}) async-start(), calls=%async_computation.32 | async-start | bytes 2359296 | tf_op jit(solution)/shard_map/reduce_scatter | solution.py:277
  915.5 80.9 %all-gather.34.cloned.1.call-start = ((), (), s32[]{:S(2)}) async-start(), calls=%async_computation.33 | async-start | bytes 2359296 | tf_op jit(solution)/shard_map/all_gather | solution.py:286
  949.1 152.4 %reduce-scatter.23.cloned.1.call-start = ((), (), s32[]{:S(2)}) async-start(), calls=%async_computation.23 | async-start | bytes 2359296 | tf_op jit(solution)/shard_map/reduce_scatter | solution.py:196
  962.9 143.2 %reduce-scatter.35.cloned.1.call-start = ((), (), s32[]{:S(2)}) async-start(), calls=%async_computation.34 | async-start | bytes 2359296 | tf_op jit(solution)/shard_map/reduce_scatter | solution.py:307
  1065.6 476.0 %all-reduce.5.cloned.1.call-start = ((), (), s32[]{:S(2)}) async-start(), calls=%async_computation.36 | async-start | bytes 28311552 | tf_op jit(solution)/shard_map/psum | solution.py:355
  (243 other events, 2915.1 us)
Sparse Core Ops, SparseCore 0:
  14.3 29.8 all-gather.13
  76.6 26.0 reduce-scatter.12
  108.1 27.2 all-gather.15
  147.2 26.0 reduce-scatter.14
  181.1 27.2 all-gather.17
  238.7 26.0 reduce-scatter.16
  269.5 27.2 all-gather.19
  309.1 26.0 reduce-scatter.18
  344.1 27.2 all-gather.21
  402.2 26.0 reduce-scatter.20
  433.6 27.2 all-gather.23
  462.8 27.1 all-gather.35
  505.1 26.0 reduce-scatter.24
  538.0 27.2 all-gather.25
  630.4 26.0 reduce-scatter.26
  668.2 27.2 all-gather.27
  710.4 26.0 reduce-scatter.28
  742.6 27.2 all-gather.29
  834.9 26.0 reduce-scatter.30
  873.4 27.2 all-gather.31
  915.7 26.0 reduce-scatter.32
  949.2 27.2 all-gather.33
  979.2 26.0 reduce-scatter.22
  1065.7 26.1 reduce-scatter.34
  1100.8 440.7 all-reduce.4
